TPU v7x, 32 devices: a whole 2x2x4 slice. The times are simulated.
32 devices in a mesh: dp: 2 (over x), expert: 16 (over z, y, core).
Axes of the slice: x: 2, y: 2, z: 4, core: 2. Of those that a mesh axis runs over, the one named last changes fastest.
Arguments:
- tokens: bfloat16 [4096, 1024], P(('dp', 'expert')), may hold values from -6 to 6
- grad_out: bfloat16 [4096, 1024], P(('dp', 'expert')), may hold values from -6 to 6
- expert_ids: int32 [4096, 8], P(('dp', 'expert')), may hold values from 0 to 15, all different within a row; in each aligned block of 128 rows (0 to 127, 128 to 255, ...) at most 72 rows name the same one
- gate_numer: int32 [4096, 8], P(('dp', 'expert')), may hold values from 1 to 16
- w_gate: bfloat16 [16, 1024, 384], P('expert', 'dp'), may hold values from -0.1875 to 0.1875
- w_up: bfloat16 [16, 1024, 384], P('expert', 'dp'), may hold values from -0.1875 to 0.1875
- w_down: bfloat16 [16, 1024, 384], P('expert', 'dp'), may hold values from -0.3125 to 0.3125
Outputs:
- grad_tokens: bfloat16 [4096, 1024], P(('dp', 'expert'))
- grad_gate: bfloat16 [16, 1024, 384], P('expert', 'dp')
- grad_up: bfloat16 [16, 1024, 384], P('expert', 'dp')
- grad_down: bfloat16 [16, 1024, 384], P('expert', 'dp')
Inputs may be any that keep to these rules, and one draw needn't show every extreme that they name: `expert_ids`: each row names 8 different experts. Within the rows of one device no expert is named more than 72 times, and in every draw some expert is named exactly 72 times within some device's rows.
All inputs are finite; a program needn't handle non-finite values.
Results may differ from a plain program's by a relative error of at most 0.0065.
Values may be sent and summed in bfloat16 or wider, within the bound.
A program may use at most 128 MiB of HBM per device.

v0:
```python
import jax
import jax.numpy as jnp
from jax import lax
from jax.sharding import PartitionSpec as P


def backward_rows(rows_in, grads_in, gate_mat, up_mat, down_mat):
    pre_gate = jnp.dot(rows_in, gate_mat, preferred_element_type=jnp.float32)
    pre_up = jnp.dot(rows_in, up_mat, preferred_element_type=jnp.float32)
    sigmoid_gate = jax.nn.sigmoid(pre_gate)
    activation = (pre_gate * sigmoid_gate * pre_up).astype(jnp.bfloat16)
    grad_act = jnp.dot(grads_in, down_mat, preferred_element_type=jnp.float32)
    grad_up = (grad_act * pre_gate * sigmoid_gate).astype(jnp.bfloat16)
    grad_gate = (grad_act * pre_up * sigmoid_gate * (1.0 + pre_gate * (1.0 - sigmoid_gate))).astype(
        jnp.bfloat16
    )
    grad_rows = jnp.einsum("rf,df->rd", grad_gate, gate_mat, preferred_element_type=jnp.float32)
    grad_rows = grad_rows + jnp.einsum(
        "rf,df->rd", grad_up, up_mat, preferred_element_type=jnp.float32
    )
    return (grad_rows.astype(jnp.bfloat16), grad_gate, grad_up, activation)


def on_device(tokens, grad_out, expert_ids, gate_numer, w_gate, w_up, w_down):
    peers = lax.axis_size("expert")
    data_groups = lax.axis_size("dp")
    tok_rows = tokens.shape[0]
    model_width = tokens.shape[1]
    top_count = expert_ids.shape[1]
    hidden_width = w_gate.shape[2]
    mean_rows = tok_rows * top_count // peers
    capacity = min(tok_rows, mean_rows + tok_rows * top_count // (8 * peers))
    pair_count = tok_rows * top_count
    slot_count = peers * capacity
    numer = gate_numer.astype(jnp.float32)
    gate = numer / jnp.sum(numer, axis=1, keepdims=True)
    scaled = (gate[:, :, None] * grad_out.astype(jnp.float32)[:, None, :]).astype(jnp.bfloat16)
    scaled = scaled.reshape(pair_count, model_width)
    flat_ids = expert_ids.reshape(-1)
    one_hot = (flat_ids[:, None] == jnp.arange(peers, dtype=jnp.int32)[None, :]).astype(
        jnp.bfloat16
    )
    pair_range = jnp.arange(pair_count, dtype=jnp.int32)
    lower = (pair_range[None, :] < pair_range[:, None]).astype(jnp.bfloat16)
    earlier = jnp.dot(lower, one_hot, preferred_element_type=jnp.float32)
    slot = jnp.sum(earlier * one_hot.astype(jnp.float32), axis=1).astype(jnp.int32)
    target = flat_ids * capacity + slot
    pair_of_slot = jnp.full((slot_count,), pair_count, jnp.int32).at[target].set(pair_range)
    token_of_slot = jnp.where(pair_of_slot < pair_count, pair_of_slot // top_count, tok_rows)
    zero_row = jnp.zeros((1, model_width), jnp.bfloat16)
    padded_tokens = jnp.concatenate([tokens, zero_row], axis=0)
    padded_scaled = jnp.concatenate([scaled, zero_row], axis=0)
    send_rows = padded_tokens[token_of_slot].reshape(peers, capacity, model_width)
    send_grads = padded_scaled[pair_of_slot].reshape(peers, capacity, model_width)
    gathered = (
        lax.all_gather(w_gate, "dp", axis=1, tiled=True),
        lax.all_gather(w_up, "dp", axis=1, tiled=True),
        lax.all_gather(w_down, "dp", axis=1, tiled=True),
    )
    gate_mat = gathered[0][0]
    up_mat = gathered[1][0]
    down_mat = gathered[2][0]
    arrived_rows, arrived_grads = (
        lax.all_to_all(send_rows, "expert", split_axis=0, concat_axis=0, tiled=True),
        lax.all_to_all(send_grads, "expert", split_axis=0, concat_axis=0, tiled=True),
    )
    rows_in = arrived_rows.reshape(slot_count, model_width)
    grads_in = arrived_grads.reshape(slot_count, model_width)
    grad_rows, grad_gate, grad_up, activation = backward_rows(
        rows_in, grads_in, gate_mat, up_mat, down_mat
    )
    returned = lax.all_to_all(
        grad_rows.reshape(peers, capacity, model_width),
        "expert",
        split_axis=0,
        concat_axis=0,
        tiled=True,
    )
    picked = returned.reshape(slot_count, model_width)[target].astype(jnp.float32)
    grad_tokens = jnp.sum(picked.reshape(tok_rows, top_count, model_width), axis=1).astype(
        jnp.bfloat16
    )
    quarter = model_width // data_groups
    term_gate = jnp.einsum(
        "rd,rf->df", rows_in, grad_gate, preferred_element_type=jnp.float32
    ).astype(jnp.bfloat16)
    term_up = jnp.einsum("rd,rf->df", rows_in, grad_up, preferred_element_type=jnp.float32).astype(
        jnp.bfloat16
    )
    term_down = jnp.einsum(
        "rd,rf->df", grads_in, activation, preferred_element_type=jnp.float32
    ).astype(jnp.bfloat16)
    stacked = jnp.stack([term_gate, term_up, term_down]).reshape(
        3, data_groups, quarter, hidden_width
    )
    arrived = lax.all_to_all(stacked, "dp", split_axis=1, concat_axis=1, tiled=True)
    summed = jnp.sum(arrived.astype(jnp.float32), axis=1).astype(jnp.bfloat16)
    return (grad_tokens, summed[0][None], summed[1][None], summed[2][None])


def solution(mesh):
    return jax.shard_map(
        on_device,
        mesh=mesh,
        in_specs=(
            P(("dp", "expert"), None),
            P(("dp", "expert"), None),
            P(("dp", "expert"), None),
            P(("dp", "expert"), None),
            P("expert", "dp", None),
            P("expert", "dp", None),
            P("expert", "dp", None),
        ),
        out_specs=(
            P(("dp", "expert"), None),
            P("expert", "dp", None),
            P("expert", "dp", None),
            P("expert", "dp", None),
        ),
        check_vma=False,
    )
```

profile of v0, /device:TPU:13, one launch (start us, length us, event | category | flops | bytes accessed | tf_op | source)
XLA Modules:
  0.0 246.2 jit_solution(5006422633957632403)
XLA Ops:
  2.9 4.3 %scatter_custom_fusion = s32[1152]{0:T(1024)S(1)} fusion(s32[1024]{0:T(1024)S(1)} %bitcast.56, s32[1024]{0:T(1024)S(1)} %iota.13, s32[]{:T(128)} %constant.12.clone.1), kind=kCustom, calls=%fused_computation.46 | custom fusion | bytes 4612 | tf_op jit(solution)/shard_map/scatter | solution.py:48
  8.3 5.0 %gather_fusion.1 = bf16[1152,1024]{1,0:T(8,128)(2,1)} fusion(bf16[129,1024]{1,0:T(8,128)(2,1)S(1)} %concatenate.8, s32[2048]{0:T(1024)S(1)} %get-tuple-element.11), kind=kCustom, calls=%fused_computation.1 | custom fusion | bytes 4723200 | tf_op jit(solution)/shard_map/gather | solution.py:53
  13.2 6.7 %all-to-all-start.1 = ((bf16[16,72,1024]{2,1,0:T(8,128)(2,1)}), bf16[16,72,1024]{2,1,0:T(8,128)(2,1)}, u32[]{:S(2)}, u32[]{:S(2)}) async-start(bf16[16,72,1024]{2,1,0:T(8,128)(2,1)} %bitcast.6), calls=%async_computation.1 | async-start | bytes 4718592 | tf_op jit(solution)/shard_map/all_to_all | solution.py:64
  20.7 5.0 %gather_fusion = bf16[1152,1024]{1,0:T(8,128)(2,1)} fusion(bf16[1025,1024]{1,0:T(8,128)(2,1)S(1)} %concatenate.7, s32[2048]{0:T(1024)S(1)} %get-tuple-element.12), kind=kCustom, calls=%fused_computation | custom fusion | bytes 4723200 | tf_op jit(solution)/shard_map/gather | solution.py:54
  25.7 47.4 %all-to-all-done.1 = bf16[16,72,1024]{2,1,0:T(8,128)(2,1)} async-done(((bf16[16,72,1024]{2,1,0:T(8,128)(2,1)}), bf16[16,72,1024]{2,1,0:T(8,128)(2,1)}, u32[]{:S(2)}, u32[]{:S(2)}) %all-to-all-start.1) | async-done | bytes 2359328 | tf_op jit(solution)/shard_map/all_to_all | solution.py:64
  73.1 5.0 %all-to-all-start = ((bf16[16,72,1024]{2,1,0:T(8,128)(2,1)}), bf16[16,72,1024]{2,1,0:T(8,128)(2,1)S(1)}, u32[]{:S(2)}, u32[]{:S(2)}) async-start(bf16[16,72,1024]{2,1,0:T(8,128)(2,1)} %bitcast.49), calls=%async_computation | async-start | bytes 4718592 | tf_op jit(solution)/shard_map/all_to_all | solution.py:65
  78.1 11.1 %all_gather.10 = bf16[1,1024,384]{2,1,0:T(8,128)(2,1)S(1)} all-gather(bf16[1,512,384]{2,1,0:T(8,128)(2,1)S(1)} %copy-done.6), channel_id=1, replica_groups=mesh['dp'=2,'expert'=16] {'dp'}, dimensions={1}, use_global_device_ids=true | all-gather | bytes 1179648 | tf_op jit(solution)/shard_map/all_gather | solution.py:57
  89.3 10.3 %all_gather.11 = bf16[1,1024,384]{2,1,0:T(8,128)(2,1)S(1)} all-gather(bf16[1,512,384]{2,1,0:T(8,128)(2,1)} %param.11), channel_id=1, replica_groups=mesh['dp'=2,'expert'=16] {'dp'}, dimensions={1}, use_global_device_ids=true | all-gather | bytes 1179648 | tf_op jit(solution)/shard_map/all_gather | solution.py:56
  99.6 9.4 %all_gather.9 = bf16[1,1024,384]{2,1,0:T(8,128)(2,1)} all-gather(bf16[1,512,384]{2,1,0:T(8,128)(2,1)S(1)} %copy-done.7), channel_id=1, replica_groups=mesh['dp'=2,'expert'=16] {'dp'}, dimensions={1}, use_global_device_ids=true | all-gather | bytes 1179648 | tf_op jit(solution)/shard_map/all_gather | solution.py:58
  109.0 4.3 %fusion.10 = f32[1152,384]{1,0:T(8,128)} fusion(bf16[1152,1024]{1,0:T(8,128)(2,1)} %bitcast.7, bf16[1,1024,384]{2,1,0:T(8,128)(2,1)S(1)} %all_gather.10), kind=kOutput, calls=%fused_computation.26 | convolution fusion | flops 905969664 | bytes 4915200 | tf_op jit(solution)/shard_map/dot_general | solution.py:9
  113.3 4.3 %fusion.7 = f32[1152,384]{1,0:T(8,128)} fusion(bf16[1152,1024]{1,0:T(8,128)(2,1)} %bitcast.7, bf16[1,1024,384]{2,1,0:T(8,128)(2,1)S(1)} %all_gather.11), kind=kOutput, calls=%fused_computation.23 | convolution fusion | flops 905969664 | bytes 4915200 | tf_op jit(solution)/shard_map/dot_general | solution.py:8
  117.6 13.5 %all-to-all-done = bf16[16,72,1024]{2,1,0:T(8,128)(2,1)S(1)} async-done(((bf16[16,72,1024]{2,1,0:T(8,128)(2,1)}), bf16[16,72,1024]{2,1,0:T(8,128)(2,1)S(1)}, u32[]{:S(2)}, u32[]{:S(2)}) %all-to-all-start) | async-done | bytes 2359328 | tf_op jit(solution)/shard_map/all_to_all | solution.py:65
  131.2 3.7 %convolution_convert_fusion = bf16[1024,384]{1,0:T(8,128)(2,1)S(1)} fusion(bf16[1152,1024]{1,0:T(8,128)(2,1)S(1)} %bitcast.51, f32[1152,384]{1,0:T(8,128)} %fusion.10, f32[1152,384]{1,0:T(8,128)} %fusion.7), kind=kOutput, calls=%fused_computation.16 | convolution fusion | flops 909017088 | bytes 6684672 | tf_op jit(solution)/shard_map/rd,rf->df/dot_general | solution.py:90
  136.8 3.8 %convolution_convert_fusion.2 = bf16[1024,384]{1,0:T(8,128)(2,1)S(1)} fusion(bf16[1152,1024]{1,0:T(8,128)(2,1)} %bitcast.7, bf16[1152,384]{1,0:T(8,128)(2,1)S(1)} %get-tuple-element.5), kind=kOutput, calls=%fused_computation.18 | convolution fusion | flops 906362880 | bytes 4030464 | tf_op jit(solution)/shard_map/rd,rf->df/dot_general | solution.py:84
  140.7 3.2 %convolution_convert_fusion.1 = bf16[1024,384]{1,0:T(8,128)(2,1)S(1)} fusion(bf16[1152,1024]{1,0:T(8,128)(2,1)} %bitcast.7, bf16[1152,384]{1,0:T(8,128)(2,1)S(1)} %get-tuple-element.4), kind=kOutput, calls=%fused_computation.17 | convolution fusion | flops 906362880 | bytes 4030464 | tf_op jit(solution)/shard_map/rd,rf->df/dot_general | solution.py:87
  145.6 3.8 %all-to-all-start.3 = ((bf16[3,2,512,384]{3,2,0,1:T(8,128)(2,1)}), bf16[3,2,512,384]{3,2,0,1:T(8,128)(2,1)S(1)}, u32[]{:S(2)}, u32[]{:S(2)}) async-start(bf16[3,2,512,384]{3,2,0,1:T(8,128)(2,1)} %pad_maximum_fusion), calls=%async_computation.3 | async-start | bytes 4718592 | tf_op jit(solution)/shard_map/all_to_all | solution.py:96
  149.4 2.9 %fusion.5 = f32[1152,1024]{1,0:T(8,128)S(1)} fusion(bf16[1152,384]{1,0:T(8,128)(2,1)} %copy-done.2, bf16[1,1024,384]{2,1,0:T(8,128)(2,1)} %copy-done.1), kind=kOutput, calls=%fused_computation.21 | convolution fusion | flops 905969664 | bytes 6389760 | tf_op jit(solution)/shard_map/rf,df->rd/dot_general | solution.py:17
  152.3 2.9 %fusion.2 = bf16[1152,1024]{1,0:T(8,128)(2,1)} fusion(f32[1152,1024]{1,0:T(8,128)S(1)} %fusion.5, bf16[1152,384]{1,0:T(8,128)(2,1)S(1)} %copy-done.4, bf16[1,1024,384]{2,1,0:T(8,128)(2,1)S(1)} %all_gather.10), kind=kOutput, calls=%fused_computation.9 | convolution fusion | flops 908328960 | bytes 8749056 | tf_op jit(solution)/shard_map/rf,df->rd/dot_general | solution.py:18
  155.2 21.8 %all-to-all-done.3 = bf16[3,2,512,384]{3,2,0,1:T(8,128)(2,1)S(1)} async-done(((bf16[3,2,512,384]{3,2,0,1:T(8,128)(2,1)}), bf16[3,2,512,384]{3,2,0,1:T(8,128)(2,1)S(1)}, u32[]{:S(2)}, u32[]{:S(2)}) %all-to-all-start.3) | async-done | bytes 2359328 | tf_op jit(solution)/shard_map/all_to_all | solution.py:96
  178.4 5.7 %all-to-all-start.2 = ((bf16[16,72,1024]{2,1,0:T(8,128)(2,1)}), bf16[16,72,1024]{2,1,0:T(8,128)(2,1)S(1)}, u32[]{:S(2)}, u32[]{:S(2)}) async-start(bf16[16,72,1024]{2,1,0:T(8,128)(2,1)} %bitcast.50), calls=%async_computation.2 | async-start | bytes 4718592 | tf_op jit(solution)/shard_map/all_to_all | solution.py:72
  184.1 2.3 reduce_sum.45
  187.5 49.7 %all-to-all-done.2 = bf16[16,72,1024]{2,1,0:T(8,128)(2,1)S(1)} async-done(((bf16[16,72,1024]{2,1,0:T(8,128)(2,1)}), bf16[16,72,1024]{2,1,0:T(8,128)(2,1)S(1)}, u32[]{:S(2)}, u32[]{:S(2)}) %all-to-all-start.2) | async-done | bytes 2359328 | tf_op jit(solution)/shard_map/all_to_all | solution.py:72
  237.1 5.4 %gather_fusion.2 = bf16[1024,1024]{1,0:T(8,128)(2,1)} fusion(bf16[1152,1024]{1,0:T(8,128)(2,1)S(1)} %bitcast.48, s32[1024]{0:T(1024)S(1)} %broadcast_clamp_fusion), kind=kCustom, calls=%fused_computation.2 | custom fusion | bytes 4198400 | tf_op jit(solution)/shard_map/gather | solution.py:79
  242.5 3.7 %bitcast_reduce_fusion = bf16[128,1024]{1,0:T(8,128)(2,1)} fusion(bf16[1024,1024]{1,0:T(8,128)(2,1)} %gather_fusion.2), kind=kLoop, calls=%fused_computation.11 | loop fusion | flops 917504 | bytes 2359296 | tf_op jit(solution)/shard_map/reduce_sum | solution.py:80
  (47 shorter events, 10.2 us)
Async XLA Ops:
  13.2 6.7 %copy-start.8 = (bf16[128,1024]{1,0:T(8,128)(2,1)S(1)}, bf16[128,1024]{1,0:T(8,128)(2,1)}, u32[]{:S(2)}) copy-start(bf16[128,1024]{1,0:T(8,128)(2,1)} %param.8) | copy-start | bytes 786436
  13.2 6.7 %copy-start.9 = (s32[128,8]{0,1:T(8,128)S(1)}, s32[128,8]{0,1:T(8,128)}, u32[]{:S(2)}) copy-start(s32[128,8]{0,1:T(8,128)} %param.10) | copy-start | bytes 12292
  13.2 59.8 %all-to-all-start.1 = ((bf16[16,72,1024]{2,1,0:T(8,128)(2,1)}), bf16[16,72,1024]{2,1,0:T(8,128)(2,1)}, u32[]{:S(2)}, u32[]{:S(2)}) async-start(bf16[16,72,1024]{2,1,0:T(8,128)(2,1)} %bitcast.6), calls=%async_computation.1 | async-start | bytes 4718592 | tf_op jit(solution)/shard_map/all_to_all | solution.py:64
  73.1 5.0 %copy-start.6 = (bf16[1,512,384]{2,1,0:T(8,128)(2,1)S(1)}, bf16[1,512,384]{2,1,0:T(8,128)(2,1)}, u32[]{:S(2)}) copy-start(bf16[1,512,384]{2,1,0:T(8,128)(2,1)} %param.12) | copy-start | bytes 1179652
  73.1 58.1 %all-to-all-start = ((bf16[16,72,1024]{2,1,0:T(8,128)(2,1)}), bf16[16,72,1024]{2,1,0:T(8,128)(2,1)S(1)}, u32[]{:S(2)}, u32[]{:S(2)}) async-start(bf16[16,72,1024]{2,1,0:T(8,128)(2,1)} %bitcast.49), calls=%async_computation | async-start | bytes 4718592 | tf_op jit(solution)/shard_map/all_to_all | solution.py:65
  78.1 21.5 %copy-start.7 = (bf16[1,512,384]{2,1,0:T(8,128)(2,1)S(1)}, bf16[1,512,384]{2,1,0:T(8,128)(2,1)}, u32[]{:S(2)}) copy-start(bf16[1,512,384]{2,1,0:T(8,128)(2,1)} %param.13) | copy-start | bytes 1179652
  99.6 13.7 %copy-start.1 = (bf16[1,1024,384]{2,1,0:T(8,128)(2,1)}, bf16[1,1024,384]{2,1,0:T(8,128)(2,1)S(1)}, u32[]{:S(2)}) copy-start(bf16[1,1024,384]{2,1,0:T(8,128)(2,1)S(1)} %all_gather.11) | copy-start | bytes 2359300
  131.2 3.7 %copy-start.5 = (bf16[1,1024,384]{2,1,0:T(8,128)(2,1)S(1)}, bf16[1,1024,384]{2,1,0:T(8,128)(2,1)}, u32[]{:S(2)}) copy-start(bf16[1,1024,384]{2,1,0:T(8,128)(2,1)} %all_gather.9) | copy-start | bytes 2359300
  131.2 3.7 %copy-start.10 = (f32[1152,384]{1,0:T(8,128)S(1)}, f32[1152,384]{1,0:T(8,128)}, u32[]{:S(2)}) copy-start(f32[1152,384]{1,0:T(8,128)} %fusion.10) | copy-start | bytes 5308420
  131.2 3.7 %copy-start.11 = (f32[1152,384]{1,0:T(8,128)S(1)}, f32[1152,384]{1,0:T(8,128)}, u32[]{:S(2)}) copy-start(f32[1152,384]{1,0:T(8,128)} %fusion.7) | copy-start | bytes 5308420
  136.8 3.9 %copy-start.2 = (bf16[1152,384]{1,0:T(8,128)(2,1)}, bf16[1152,384]{1,0:T(8,128)(2,1)S(1)}, u32[]{:S(2)}) copy-start(bf16[1152,384]{1,0:T(8,128)(2,1)S(1)} %get-tuple-element.5) | copy-start | bytes 2654212
  136.8 3.9 %copy-start.3 = (bf16[1152,384]{1,0:T(8,128)(2,1)}, bf16[1152,384]{1,0:T(8,128)(2,1)S(1)}, u32[]{:S(2)}) copy-start(bf16[1152,384]{1,0:T(8,128)(2,1)S(1)} %get-tuple-element.4) | copy-start | bytes 2654212
  145.6 31.4 %all-to-all-start.3 = ((bf16[3,2,512,384]{3,2,0,1:T(8,128)(2,1)}), bf16[3,2,512,384]{3,2,0,1:T(8,128)(2,1)S(1)}, u32[]{:S(2)}, u32[]{:S(2)}) async-start(bf16[3,2,512,384]{3,2,0,1:T(8,128)(2,1)} %pad_maximum_fusion), calls=%async_computation.3 | async-start | bytes 4718592 | tf_op jit(solution)/shard_map/all_to_all | solution.py:96
  149.4 2.9 %copy-start.4 = (bf16[1152,384]{1,0:T(8,128)(2,1)S(1)}, bf16[1152,384]{1,0:T(8,128)(2,1)}, u32[]{:S(2)}) copy-start(bf16[1152,384]{1,0:T(8,128)(2,1)} %copy-done.3) | copy-start | bytes 2654212
  177.0 1.4 copy-start
  178.4 58.8 %all-to-all-start.2 = ((bf16[16,72,1024]{2,1,0:T(8,128)(2,1)}), bf16[16,72,1024]{2,1,0:T(8,128)(2,1)S(1)}, u32[]{:S(2)}, u32[]{:S(2)}) async-start(bf16[16,72,1024]{2,1,0:T(8,128)(2,1)} %bitcast.50), calls=%async_computation.2 | async-start | bytes 4718592 | tf_op jit(solution)/shard_map/all_to_all | solution.py:72
where the time goes:
time: 247 us; the launch traced here: 246 us
  waiting for transfers between devices  132 us (53%)
  blocking collectives  30.9 us (13%)
  matrix products  27.4 us (11%)
  local copies, waits for them, and re-layouts  24.6 us (10%)
  starting transfers between devices  21.3 us (9%)
  other arithmetic  8.85 us (4%)
    all_to_all x1, waiting for transfers between devices, on_device(): lax.all_to_all(grad_rows.reshape(peers, capacity, model_width), 'expert',...  49.7 us
    all_to_all x1, waiting for transfers between devices, on_device(): lax.all_to_all(send_rows, 'expert', split_axis=0, concat_axis=0, tiled=True)  47.4 us
    all_to_all x1, waiting for transfers between devices, on_device(): lax.all_to_all(stacked, 'dp', split_axis=1, concat_axis=1, tiled=True)  21.8 us
    all_to_all x1, waiting for transfers between devices, on_device(): lax.all_to_all(send_grads, 'expert', split_axis=0, concat_axis=0, tiled=T...  13.5 us
    all_gather x1, blocking collectives, on_device(): lax.all_gather(w_up, 'dp', axis=1, tiled=True)  11.1 us
    all_gather x1, blocking collectives, on_device(): lax.all_gather(w_gate, 'dp', axis=1, tiled=True)  10.3 us
    all_gather x1, blocking collectives, on_device(): lax.all_gather(w_down, 'dp', axis=1, tiled=True)  9.45 us
    all_to_all x1, starting transfers between devices, on_device(): lax.all_to_all(send_rows, 'expert', split_axis=0, concat_axis=0, tiled=True)  6.69 us
  transfers between devices with their start and end apart: 4, of which 4 were waited for; matrix products, arithmetic and copies ran while one was open for 10% of the time, Pallas kernels for 0%

commit v1 on v0

--- a/solution.py
+++ b/solution.py
@@ -1,7 +1,15 @@
+import functools
+
 import jax
 import jax.numpy as jnp
 from jax import lax
+from jax.experimental import pallas as pl
+from jax.experimental.pallas import tpu as pltpu
 from jax.sharding import PartitionSpec as P
+
+MESH = pl.DeviceIdType.MESH
+F32 = jnp.float32
+BF16 = jnp.bfloat16
 
 
 def backward_rows(rows_in, grads_in, gate_mat, up_mat, down_mat):
@@ -21,7 +29,7 @@
     return (grad_rows.astype(jnp.bfloat16), grad_gate, grad_up, activation)
 
 
-def on_device(tokens, grad_out, expert_ids, gate_numer, w_gate, w_up, w_down):
+def on_device_routed(tokens, grad_out, expert_ids, gate_numer, w_gate, w_up, w_down):
     peers = lax.axis_size("expert")
     data_groups = lax.axis_size("dp")
     tok_rows = tokens.shape[0]
@@ -98,9 +106,292 @@
     return (grad_tokens, summed[0][None], summed[1][None], summed[2][None])
 
 
+def contract_rows(lhs, rhs):
+    return lax.dot_general(lhs, rhs, (((0,), (0,)), ((), ())), preferred_element_type=F32)
+
+
+def layer_kernel(
+    chips, tok_ref, grad_ref, num_ref, wg_ref, wu_ref, wd_ref,
+    out_tok, out_gate, out_up, out_down,
+    xbuf, gbuf, nbuf, cbuf, sbuf, obuf, rbuf, wgu, wdn, acc_gu, acc_d, pbuf, qbuf, scaled, grads,
+    w_send, w_recv, ring_send, ring_recv, sib_send, sib_recv,
+    row_send, row_recv, sum_send, sum_recv, part_send, part_recv,
+):
+    half_ring = chips // 2
+    group = lax.axis_index("dp")
+    me = lax.axis_index("expert")
+    core = lax.rem(me, 2)
+    chip = lax.div(me, 2)
+    lane = lax.rem(chip, 2)
+    depth = lax.div(chip, 2)
+    pos = jnp.where(lane == 0, depth, chips - 1 - depth)
+
+    def device_at(ring_pos):
+        far = ring_pos >= half_ring
+        along = jnp.where(far, chips - 1 - ring_pos, ring_pos)
+        return along * 4 + jnp.where(far, 2, 0) + core
+
+    def ring(offset):
+        return lax.rem(pos + offset + chips, chips)
+
+    right = (group, device_at(ring(1)))
+    left = (group, device_at(ring(-1)))
+    sibling = (group, me + 1 - 2 * core)
+    other = (1 - group, me)
+    flows = (right, left)
+
+    barrier = pltpu.get_barrier_semaphore()
+    for target in (right, left, sibling, other):
+        pl.semaphore_signal(barrier, inc=1, device_id=target, device_id_type=MESH)
+    pl.semaphore_wait(barrier, 4)
+
+    started = []
+
+    def copy(src, dst, send, recv, target):
+        return pltpu.make_async_remote_copy(
+            src_ref=src, dst_ref=dst, send_sem=send, recv_sem=recv,
+            device_id=target, device_id_type=MESH,
+        )
+
+    def start(*args):
+        op = copy(*args)
+        op.start()
+        started.append(op)
+
+    share = wg_ref.shape[0]
+    hidden = wg_ref.shape[1]
+    own_rows = pl.ds(pl.multiple_of(group * share, share), share)
+    other_rows = pl.ds(pl.multiple_of((1 - group) * share, share), share)
+
+    own = (tok_ref, grad_ref, num_ref)
+    bufs = (xbuf, gbuf, nbuf)
+
+    def weight_places(rows):
+        return (
+            wgu.at[rows, pl.ds(0, hidden)],
+            wgu.at[rows, pl.ds(hidden, hidden)],
+            wdn.at[rows, :],
+        )
+
+    for a in (0, 2, 1):
+        for f in range(2):
+            start(own[a], bufs[a].at[pos, core], ring_send.at[a, f, 0], ring_recv.at[a, f, 0], flows[f])
+    for k, ref in enumerate((wg_ref, wu_ref, wd_ref)):
+        start(ref, weight_places(own_rows)[k], w_send.at[k], w_recv.at[k], other)
+    for a in (0, 2, 1):
+        start(own[a], bufs[a].at[pos, core], sib_send.at[a, 0], sib_recv.at[a, 0], sibling)
+    for a in range(3):
+        bufs[a][pos, core] = own[a][...]
+    wgu[own_rows, pl.ds(0, hidden)] = wg_ref[...]
+    wgu[own_rows, pl.ds(hidden, hidden)] = wu_ref[...]
+    wdn[own_rows, :] = wd_ref[...]
+    acc_gu[...] = jnp.zeros_like(acc_gu)
+    acc_d[...] = jnp.zeros_like(acc_d)
+
+    def part(a, q, c, step, f):
+        ref = bufs[a].at[q, c]
+        if step == half_ring:
+            n = bufs[a].shape[2] // 2
+            ref = bufs[a].at[q, c, pl.ds(f * n, n)]
+        return ref
+
+    def arrive(a, step):
+        for f in range(2):
+            q = ring(-step if f == 0 else step)
+            ref = part(a, q, core, step, f)
+            copy(ref, ref, ring_send.at[a, f, step - 1], ring_recv.at[a, f, step - 1], flows[f]).wait_recv()
+            if step < half_ring:
+                ref2 = part(a, q, core, step + 1, f)
+                start(ref2, ref2, ring_send.at[a, f, step], ring_recv.at[a, f, step], flows[f])
+            k = 2 * step - 1 + f
+            start(ref, ref, sib_send.at[a, k], sib_recv.at[a, k], sibling)
+
+    def arrive_sibling(step):
+        for a in range(3):
+            for f in range(2 if step else 1):
+                q = ring(-step if f == 0 else step)
+                ref = part(a, q, 1 - core, step, f)
+                k = 2 * step - 1 + f if step else 0
+                copy(ref, ref, sib_send.at[a, k], sib_recv.at[a, k], sibling).wait_recv()
+
+    rows = 2 * tok_ref.shape[0]
+    width = tok_ref.shape[1]
+    block = tok_ref.shape[0]
+    experts = num_ref.shape[0] // 2
+    row_ids = lax.broadcasted_iota(jnp.int32, (2 * experts, 256), 0)
+    col_ids = lax.broadcasted_iota(jnp.int32, (2 * experts, 256), 1)
+    wanted = jnp.where(col_ids < 128, me, experts)
+    select = jnp.where(row_ids == wanted, 1.0, 0.0).astype(BF16)
+
+    def chunk_ring(i):
+        return lax.rem(pos + (1 - 2 * (i % 2)) * ((i + 1) // 2) + chips, chips)
+
+    def chunk(i, carry):
+        away = lax.div(i + 1, 2)
+        q = lax.rem(pos + (1 - 2 * lax.rem(i, 2)) * away + chips, chips)
+        for b in range(2):
+            both = contract_rows(nbuf[q, b], select)
+            gate = both[:, :128] / both[:, 128:]
+            for k in range(width // 128):
+                cols = pl.ds(k * 128, 128)
+                scaled[pl.ds(b * block, block), cols] = (
+                    gate * gbuf[q, b, :, cols].astype(F32)
+                ).astype(BF16)
+        x = xbuf[q].reshape(rows, width)
+        pre = jnp.dot(x, wgu[...], preferred_element_type=F32)
+        pre_gate = pre[:, :hidden]
+        pre_up = pre[:, hidden:]
+        grad_act = jnp.dot(scaled[...], wdn[...], preferred_element_type=F32)
+        sig = jax.nn.sigmoid(pre_gate)
+        silu = pre_gate * sig
+        act = (silu * pre_up).astype(BF16)
+        grads[:, pl.ds(hidden, hidden)] = (grad_act * silu).astype(BF16)
+        grads[:, pl.ds(0, hidden)] = (
+            grad_act * pre_up * sig * (1.0 + pre_gate * (1.0 - sig))
+        ).astype(BF16)
+        back = lax.dot_general(
+            grads[...], wgu[...], (((1,), (1,)), ((), ())), preferred_element_type=F32
+        )
+        cbuf[q] = back.astype(BF16).reshape(2, block, width)
+        acc_gu[...] += contract_rows(x, grads[...])
+        acc_d[...] += contract_rows(scaled[...], act)
+        return carry
+
+    def chunks(first, last):
+        lax.fori_loop(first, last, chunk, 0)
+        for i in range(first, last):
+            q = chunk_ring(i)
+            start(cbuf.at[q, 1 - core], sbuf.at[q], row_send.at[i], row_recv.at[i], sibling)
+
+    for step in range(1, half_ring - 1):
+        for a in (0, 2, 1):
+            arrive(a, step)
+    for k, ref in enumerate(weight_places(other_rows)):
+        copy(ref, ref, w_send.at[k], w_recv.at[k], other).wait_recv()
+    for step in range(half_ring - 1):
+        arrive_sibling(step)
+    chunks(0, 3)
+    arrive(0, half_ring - 1)
+    chunks(3, 4)
+    arrive(2, half_ring - 1)
+    arrive(1, half_ring - 1)
+    arrive_sibling(half_ring - 1)
+    chunks(4, 7)
+    for a in (0, 2, 1):
+        arrive(a, half_ring)
+    arrive_sibling(half_ring)
+    chunks(7, 8)
+
+    def term(k, where):
+        if k == 2:
+            return acc_d[where, :].astype(BF16)
+        return acc_gu[where, pl.ds(k * hidden, hidden)].astype(BF16)
+
+    for k in range(3):
+        pbuf[k] = term(k, other_rows)
+        start(pbuf.at[k], qbuf.at[k], part_send.at[k], part_recv.at[k], other)
+
+    half = block // 2
+    got_rows = set()
+
+    def row_sum(q_off, h):
+        off = q_off
+        i = 0 if off == 0 else (2 * off if off > 0 else -2 * off - 1)
+        i = min(i, chips - 1)
+        q = ring(off)
+        if i not in got_rows:
+            got_rows.add(i)
+            copy(sbuf.at[q], sbuf.at[q], row_send.at[i], row_recv.at[i], sibling).wait_recv()
+        at = pl.ds(h * half, half)
+        return cbuf[q, core, at].astype(F32) + sbuf[q, at].astype(F32)
+
+    def order(f):
+        listed = [(half_ring, f)]
+        for d in range(half_ring - 1, 0, -1):
+            listed += [(d, 1 - f), (d, f)]
+        return listed
+
+    def incoming(f, d, h):
+        j = order(f).index((d + 1, h))
+        ref = rbuf.at[f, j]
+        copy(ref, ref, sum_send.at[f, j], sum_recv.at[f, j], flows[f]).wait_recv()
+        return rbuf[f, j].astype(F32)
+
+    for j in range(len(order(0))):
+        for f in range(2):
+            d, h = order(f)[j]
+            value = row_sum(d if f == 0 else -d, h)
+            if (d + 1, h) in order(f):
+                value = value + incoming(f, d, h)
+            obuf[f, j] = value.astype(BF16)
+            start(obuf.at[f, j], rbuf.at[f, j], sum_send.at[f, j], sum_recv.at[f, j], flows[f])
+    for h in range(2):
+        value = row_sum(0, h) + incoming(0, 0, h) + incoming(1, 0, h)
+        out_tok[pl.ds(h * half, half), :] = value.astype(BF16)
+
+    for k, out in enumerate((out_gate, out_up, out_down)):
+        copy(qbuf.at[k], qbuf.at[k], part_send.at[k], part_recv.at[k], other).wait_recv()
+        out[...] = (term(k, own_rows).astype(F32) + qbuf[k].astype(F32)).astype(BF16)
+    for op in started:
+        op.wait_send()
+
+
+def on_device_dense(tokens, grad_out, expert_ids, gate_numer, w_gate, w_up, w_down):
+    peers = lax.axis_size("expert")
+    chips = peers // 2
+    block, width = tokens.shape
+    share, hidden = w_gate.shape[1:]
+    depth = share * lax.axis_size("dp")
+    hit = expert_ids.T[None, :, :] == jnp.arange(peers, dtype=jnp.int32)[:, None, None]
+    by_expert = jnp.sum(jnp.where(hit, gate_numer.T[None], 0), axis=1)
+    total = jnp.broadcast_to(jnp.sum(gate_numer, axis=1)[None, :], (peers, block))
+    numbers = jnp.concatenate([by_expert, total], axis=0).astype(BF16)
+
+    messages = chips - 1
+    dma = pltpu.SemaphoreType.DMA
+    vmem = pl.BlockSpec(memory_space=pltpu.VMEM)
+    outs = pl.pallas_call(
+        functools.partial(layer_kernel, chips),
+        out_shape=(jax.ShapeDtypeStruct((block, width), BF16),)
+        + (jax.ShapeDtypeStruct((share, hidden), BF16),) * 3,
+        in_specs=[vmem] * 6,
+        out_specs=(vmem,) * 4,
+        scratch_shapes=[
+            pltpu.VMEM((chips, 2, block, width), BF16),
+            pltpu.VMEM((chips, 2, block, width), BF16),
+            pltpu.VMEM((chips, 2, 2 * peers, block), BF16),
+            pltpu.VMEM((chips, 2, block, width), BF16),
+            pltpu.VMEM((chips, block, width), BF16),
+            pltpu.VMEM((2, messages, block // 2, width), BF16),
+            pltpu.VMEM((2, messages, block // 2, width), BF16),
+            pltpu.VMEM((depth, 2 * hidden), BF16),
+            pltpu.VMEM((depth, hidden), BF16),
+            pltpu.VMEM((depth, 2 * hidden), F32),
+            pltpu.VMEM((depth, hidden), F32),
+            pltpu.VMEM((3, share, hidden), BF16),
+            pltpu.VMEM((3, share, hidden), BF16),
+            pltpu.VMEM((2 * block, width), BF16),
+            pltpu.VMEM((2 * block, 2 * hidden), BF16),
+            dma((3,)), dma((3,)),
+            dma((3, 2, chips // 2)), dma((3, 2, chips // 2)),
+            dma((3, chips + 1)), dma((3, chips + 1)),
+            dma((chips,)), dma((chips,)),
+            dma((2, messages)), dma((2, messages)),
+            dma((3,)), dma((3,)),
+        ],
+        compiler_params=pltpu.CompilerParams(
+            collective_id=0, has_side_effects=True, vmem_limit_bytes=56 * 1024 * 1024
+        ),
+        cost_estimate=pl.CostEstimate(
+            flops=16 * peers * block * width * hidden, bytes_accessed=8 * block * width, transcendentals=0
+        ),
+    )(tokens, grad_out, numbers, w_gate[0], w_up[0], w_down[0])
+    return (outs[0],) + tuple(value[None] for value in outs[1:])
+
+
 def solution(mesh):
     return jax.shard_map(
-        on_device,
+        on_device_dense if mesh.shape["expert"] == 16 else on_device_routed,
         mesh=mesh,
         in_specs=(
             P(("dp", "expert"), None),

time: 247 us -> 92.2 us (0.37)
  the two profiles are of different devices: /device:TPU:13 before, /device:TPU:0 now
where the time goes in v1:
time: 92.2 us; the launch traced here: 91.9 us
  Pallas kernels  84.4 us (92%)
  local copies, waits for them, and re-layouts  6.09 us (7%)
    pallas_call x1, Pallas kernels, on_device_dense(): pl.pallas_call(functools.partial(layer_kernel, chips), out_shape=(jax.Sha...  84.4 us
    unnamed x14, local copies, waits for them, and re-layouts  6.09 us

profile of v1, /device:TPU:0, one launch (start us, length us, event | category | flops | bytes accessed | tf_op | source)
XLA Modules:
  0.0 91.9 jit_solution(6161948955739530384)
XLA Ops:
  0.6 0.0 copy-start.3
  0.6 0.7 copy-done.3
  1.3 0.0 copy-start.4
  1.4 0.7 copy-done.4
  2.1 0.6 pad_maximum_fusion.num_ref
  2.7 84.4 %shard_map.102 = (bf16[128,1024]{1,0:T(8,128)(2,1)}, bf16[512,384]{1,0:T(8,128)(2,1)}, bf16[512,384]{1,0:T(8,128)(2,1)}, bf16[512,384]{1,0:T(8,128)(2,1)}) custom-call(bf16[128,1024]{1,0:T(8,128)(2,1)} %tok_ref.1, bf16[128,1024]{1,0:T(8,128)(2,1)} %grad_ref.1, bf16[32,128]{1,0:T(8,128)(2,1)} %pad_maximum_fusion.num_ref, bf16[512,384]{1,0:T(8,128)(2,1)} %bitcast.13, ...), custom_call_target="tpu_custom_call" | custom-call | flops 12884901888 | bytes 1048576 | tf_op jit(solution)/shard_map/pallas_call | solution.py:353
  87.1 0.0 copy-start.2
  87.1 1.7 %copy.15 = bf16[128,1024]{1,0:T(8,128)(2,1)} copy(bf16[128,1024]{1,0:T(8,128)(2,1)} %get-tuple-element.16) | data formatting | bytes 524288
  88.8 0.0 copy-done.2
  88.8 0.0 copy-start.1
  88.8 0.7 copy.16
  89.6 0.4 copy-done.1
  90.0 0.0 copy-start
  90.0 0.7 copy.17
  90.7 0.4 copy-done
  91.1 0.7 copy.18
  (5 shorter events, 0.1 us)
Async XLA Ops:
  0.6 0.7 copy-start.3
  1.3 0.7 copy-start.4
  87.1 1.7 %copy-start.2 = (bf16[512,384]{1,0:T(8,128)(2,1)S(1)}, bf16[512,384]{1,0:T(8,128)(2,1)}, u32[]{:S(2)}) copy-start(bf16[512,384]{1,0:T(8,128)(2,1)} %get-tuple-element.9) | copy-start | bytes 1179652
  88.8 1.1 %copy-start.1 = (bf16[512,384]{1,0:T(8,128)(2,1)S(1)}, bf16[512,384]{1,0:T(8,128)(2,1)}, u32[]{:S(2)}) copy-start(bf16[512,384]{1,0:T(8,128)(2,1)} %get-tuple-element.10) | copy-start | bytes 1179652
  90.0 1.1 %copy-start = (bf16[512,384]{1,0:T(8,128)(2,1)S(1)}, bf16[512,384]{1,0:T(8,128)(2,1)}, u32[]{:S(2)}) copy-start(bf16[512,384]{1,0:T(8,128)(2,1)} %get-tuple-element.11) | copy-start | bytes 1179652

commit v2 on v1

--- a/solution.py
+++ b/solution.py
@@ -113,7 +113,8 @@
 def layer_kernel(
     chips, tok_ref, grad_ref, num_ref, wg_ref, wu_ref, wd_ref,
     out_tok, out_gate, out_up, out_down,
-    xbuf, gbuf, nbuf, cbuf, sbuf, obuf, rbuf, wgu, wdn, acc_gu, acc_d, pbuf, qbuf, scaled, grads,
+    xbuf, gbuf, nbuf, cbuf, sbuf, obuf, rbuf, wgu, wdn, acc_gu, acc_d, pbuf, qbuf, scaled, grads, acts,
+    pre_buf, ga_buf,
     w_send, w_recv, ring_send, ring_recv, sib_send, sib_recv,
     row_send, row_recv, sum_send, sum_recv, part_send, part_recv,
 ):
@@ -160,8 +161,12 @@
 
     share = wg_ref.shape[0]
     hidden = wg_ref.shape[1]
-    own_rows = pl.ds(pl.multiple_of(group * share, share), share)
-    other_rows = pl.ds(pl.multiple_of((1 - group) * share, share), share)
+    block, width = tok_ref.shape
+    own_at = pl.ds(pl.multiple_of(group * share, share), share)
+    other_at = pl.ds(pl.multiple_of((1 - group) * share, share), share)
+
+    def slot(f, d):
+        return 0 if d == 0 else min(2 * d - 1 + f, chips - 1)
 
     own = (tok_ref, grad_ref, num_ref)
     bufs = (xbuf, gbuf, nbuf)
@@ -175,135 +180,179 @@
 
     for a in (0, 2, 1):
         for f in range(2):
-            start(own[a], bufs[a].at[pos, core], ring_send.at[a, f, 0], ring_recv.at[a, f, 0], flows[f])
+            start(own[a], bufs[a].at[slot(f, 1), core], ring_send.at[a, f, 0], ring_recv.at[a, f, 0], flows[f])
     for k, ref in enumerate((wg_ref, wu_ref, wd_ref)):
-        start(ref, weight_places(own_rows)[k], w_send.at[k], w_recv.at[k], other)
+        start(ref, weight_places(own_at)[k], w_send.at[k], w_recv.at[k], other)
     for a in (0, 2, 1):
-        start(own[a], bufs[a].at[pos, core], sib_send.at[a, 0], sib_recv.at[a, 0], sibling)
+        start(own[a], bufs[a].at[0, core], sib_send.at[a, 0], sib_recv.at[a, 0], sibling)
     for a in range(3):
-        bufs[a][pos, core] = own[a][...]
-    wgu[own_rows, pl.ds(0, hidden)] = wg_ref[...]
-    wgu[own_rows, pl.ds(hidden, hidden)] = wu_ref[...]
-    wdn[own_rows, :] = wd_ref[...]
-    acc_gu[...] = jnp.zeros_like(acc_gu)
-    acc_d[...] = jnp.zeros_like(acc_d)
-
-    def part(a, q, c, step, f):
-        ref = bufs[a].at[q, c]
+        bufs[a][0, core] = own[a][...]
+    wgu[own_at, pl.ds(0, hidden)] = wg_ref[...]
+    wgu[own_at, pl.ds(hidden, hidden)] = wu_ref[...]
+    wdn[own_at, :] = wd_ref[...]
+
+    def part(a, s, c, step, f):
         if step == half_ring:
             n = bufs[a].shape[2] // 2
-            ref = bufs[a].at[q, c, pl.ds(f * n, n)]
-        return ref
+            return bufs[a].at[s, c, pl.ds(f * n, n)]
+        return bufs[a].at[s, c]
 
     def arrive(a, step):
         for f in range(2):
-            q = ring(-step if f == 0 else step)
-            ref = part(a, q, core, step, f)
+            ref = part(a, slot(f, step), core, step, f)
             copy(ref, ref, ring_send.at[a, f, step - 1], ring_recv.at[a, f, step - 1], flows[f]).wait_recv()
             if step < half_ring:
-                ref2 = part(a, q, core, step + 1, f)
-                start(ref2, ref2, ring_send.at[a, f, step], ring_recv.at[a, f, step], flows[f])
+                src = part(a, slot(f, step), core, step + 1, f)
+                dst = part(a, slot(f, step + 1), core, step + 1, f)
+                start(src, dst, ring_send.at[a, f, step], ring_recv.at[a, f, step], flows[f])
             k = 2 * step - 1 + f
             start(ref, ref, sib_send.at[a, k], sib_recv.at[a, k], sibling)
 
-    def arrive_sibling(step):
-        for a in range(3):
+    def arrive_sibling(step, arrays=(0, 1, 2)):
+        for a in arrays:
             for f in range(2 if step else 1):
-                q = ring(-step if f == 0 else step)
-                ref = part(a, q, 1 - core, step, f)
+                ref = part(a, slot(f, step), 1 - core, step, f)
                 k = 2 * step - 1 + f if step else 0
                 copy(ref, ref, sib_send.at[a, k], sib_recv.at[a, k], sibling).wait_recv()
 
-    rows = 2 * tok_ref.shape[0]
-    width = tok_ref.shape[1]
-    block = tok_ref.shape[0]
+    per_slot = 2 * block
     experts = num_ref.shape[0] // 2
     row_ids = lax.broadcasted_iota(jnp.int32, (2 * experts, 256), 0)
     col_ids = lax.broadcasted_iota(jnp.int32, (2 * experts, 256), 1)
     wanted = jnp.where(col_ids < 128, me, experts)
     select = jnp.where(row_ids == wanted, 1.0, 0.0).astype(BF16)
 
-    def chunk_ring(i):
-        return lax.rem(pos + (1 - 2 * (i % 2)) * ((i + 1) // 2) + chips, chips)
-
-    def chunk(i, carry):
-        away = lax.div(i + 1, 2)
-        q = lax.rem(pos + (1 - 2 * lax.rem(i, 2)) * away + chips, chips)
-        for b in range(2):
-            both = contract_rows(nbuf[q, b], select)
-            gate = both[:, :128] / both[:, 128:]
-            for k in range(width // 128):
-                cols = pl.ds(k * 128, 128)
-                scaled[pl.ds(b * block, block), cols] = (
-                    gate * gbuf[q, b, :, cols].astype(F32)
-                ).astype(BF16)
-        x = xbuf[q].reshape(rows, width)
-        pre = jnp.dot(x, wgu[...], preferred_element_type=F32)
+    def span(slots):
+        return pl.ds(slots[0] * per_slot, len(slots) * per_slot)
+
+    def tokens_of(slots, cols=slice(None)):
+        return xbuf[slots[0] : slots[-1] + 1, :, :, cols].reshape(len(slots) * per_slot, -1)
+
+    def scale(slots):
+        for s in slots:
+            for b in range(2):
+                both = contract_rows(nbuf[s, b], select)
+                gate = both[:, :128] / both[:, 128:]
+                for k in range(width // 128):
+                    cols = pl.ds(k * 128, 128)
+                    scaled[pl.ds(s * per_slot + b * block, block), cols] = (
+                        gate * gbuf[s, b, :, cols].astype(F32)
+                    ).astype(BF16)
+
+    def pre_part(slots, at):
+        x = tokens_of(slots, at)
+        return jnp.dot(x, wgu[at, :], preferred_element_type=F32)
+
+    def ga_part(slots, at):
+        return jnp.dot(scaled[span(slots), at], wdn[at, :], preferred_element_type=F32)
+
+    def pointwise(slots, pre, grad_act):
+        where = span(slots)
         pre_gate = pre[:, :hidden]
         pre_up = pre[:, hidden:]
-        grad_act = jnp.dot(scaled[...], wdn[...], preferred_element_type=F32)
         sig = jax.nn.sigmoid(pre_gate)
         silu = pre_gate * sig
-        act = (silu * pre_up).astype(BF16)
-        grads[:, pl.ds(hidden, hidden)] = (grad_act * silu).astype(BF16)
-        grads[:, pl.ds(0, hidden)] = (
+        acts[where, :] = (silu * pre_up).astype(BF16)
+        grads[where, pl.ds(hidden, hidden)] = (grad_act * silu).astype(BF16)
+        grads[where, pl.ds(0, hidden)] = (
             grad_act * pre_up * sig * (1.0 + pre_gate * (1.0 - sig))
         ).astype(BF16)
-        back = lax.dot_general(
-            grads[...], wgu[...], (((1,), (1,)), ((), ())), preferred_element_type=F32
+
+    def back(slots):
+        rows = lax.dot_general(
+            grads[span(slots), :], wgu[...], (((1,), (1,)), ((), ())), preferred_element_type=F32
         )
-        cbuf[q] = back.astype(BF16).reshape(2, block, width)
-        acc_gu[...] += contract_rows(x, grads[...])
-        acc_d[...] += contract_rows(scaled[...], act)
-        return carry
-
-    def chunks(first, last):
-        lax.fori_loop(first, last, chunk, 0)
-        for i in range(first, last):
-            q = chunk_ring(i)
-            start(cbuf.at[q, 1 - core], sbuf.at[q], row_send.at[i], row_recv.at[i], sibling)
-
-    for step in range(1, half_ring - 1):
-        for a in (0, 2, 1):
-            arrive(a, step)
-    for k, ref in enumerate(weight_places(other_rows)):
+        cbuf[slots[0] : slots[-1] + 1] = rows.astype(BF16).reshape(len(slots), 2, block, width)
+        for s in slots:
+            start(cbuf.at[s, 1 - core], sbuf.at[s], row_send.at[s], row_recv.at[s], sibling)
+
+    def add_terms(slots, first=False):
+        where = span(slots)
+        gu = contract_rows(tokens_of(slots, other_at), grads[where, :])
+        dn = contract_rows(scaled[where, other_at], acts[where, :])
+        if first:
+            acc_gu[...] = gu
+            acc_d[...] = dn
+        else:
+            acc_gu[...] += gu
+            acc_d[...] += dn
+
+    def rest(slots, first=False):
+        pointwise(slots, pre_buf[span(slots), :], ga_buf[span(slots), :])
+        back(slots)
+        add_terms(slots, first)
+
+    def wait_weight(k):
+        ref = weight_places(other_at)[k]
         copy(ref, ref, w_send.at[k], w_recv.at[k], other).wait_recv()
-    for step in range(half_ring - 1):
-        arrive_sibling(step)
-    chunks(0, 3)
-    arrive(0, half_ring - 1)
-    chunks(3, 4)
-    arrive(2, half_ring - 1)
-    arrive(1, half_ring - 1)
-    arrive_sibling(half_ring - 1)
-    chunks(4, 7)
+
+    slots_a, slots_b, slots_c, slots_d, slots_e = [0], [1, 2], [3, 4], [5, 6], [7]
+    everything = slice(None)
+
+    arrive_sibling(0)
+    scale(slots_a)
+    pre_buf[span(slots_a), :] = pre_part(slots_a, own_at)
+    ga_buf[span(slots_a), :] = ga_part(slots_a, own_at)
+    arrive(0, 1)
+    arrive_sibling(1, (0,))
+    pre_buf[span(slots_b), :] = pre_part(slots_b, own_at)
+    arrive(2, 1)
+    arrive(1, 1)
+    arrive_sibling(1, (1, 2))
+    scale(slots_b)
+    ga_buf[span(slots_b), :] = ga_part(slots_b, own_at)
+    arrive(0, 2)
+    arrive_sibling(2, (0,))
+    wait_weight(0)
+    wait_weight(1)
+    pre_buf[span(slots_a), :] += pre_part(slots_a, other_at)
+    pre_buf[span(slots_b), :] += pre_part(slots_b, other_at)
+    arrive(2, 2)
+    arrive(1, 2)
+    pre_buf[span(slots_c), :] = pre_part(slots_c, everything)
+    wait_weight(2)
+    ga_buf[span(slots_a), :] += ga_part(slots_a, other_at)
+    rest(slots_a, True)
+    ga_buf[span(slots_b), :] += ga_part(slots_b, other_at)
+    arrive(0, 3)
+    rest(slots_b)
+    arrive_sibling(2, (1, 2))
+    scale(slots_c)
+    ga_buf[span(slots_c), :] = ga_part(slots_c, everything)
+    arrive(2, 3)
+    arrive(1, 3)
+    rest(slots_c)
+    arrive_sibling(3)
+    scale(slots_d)
+    pointwise(slots_d, pre_part(slots_d, everything), ga_part(slots_d, everything))
     for a in (0, 2, 1):
-        arrive(a, half_ring)
-    arrive_sibling(half_ring)
-    chunks(7, 8)
-
-    def term(k, where):
+        arrive(a, 4)
+    back(slots_d)
+    add_terms(slots_d)
+    arrive_sibling(4)
+    scale(slots_e)
+    pointwise(slots_e, pre_part(slots_e, everything), ga_part(slots_e, everything))
+    back(slots_e)
+
+    last = span(slots_e)
+    for k in range(3):
         if k == 2:
-            return acc_d[where, :].astype(BF16)
-        return acc_gu[where, pl.ds(k * hidden, hidden)].astype(BF16)
-
-    for k in range(3):
-        pbuf[k] = term(k, other_rows)
+            value = acc_d[...] + contract_rows(scaled[last, other_at], acts[last, :])
+        else:
+            cols = pl.ds(k * hidden, hidden)
+            value = acc_gu[:, cols] + contract_rows(tokens_of(slots_e, other_at), grads[last, cols])
+        pbuf[k] = value.astype(BF16)
         start(pbuf.at[k], qbuf.at[k], part_send.at[k], part_recv.at[k], other)
 
     half = block // 2
     got_rows = set()
 
-    def row_sum(q_off, h):
-        off = q_off
-        i = 0 if off == 0 else (2 * off if off > 0 else -2 * off - 1)
-        i = min(i, chips - 1)
-        q = ring(off)
-        if i not in got_rows:
-            got_rows.add(i)
-            copy(sbuf.at[q], sbuf.at[q], row_send.at[i], row_recv.at[i], sibling).wait_recv()
+    def row_sum(s, h):
+        if s not in got_rows:
+            got_rows.add(s)
+            copy(sbuf.at[s], sbuf.at[s], row_send.at[s], row_recv.at[s], sibling).wait_recv()
         at = pl.ds(h * half, half)
-        return cbuf[q, core, at].astype(F32) + sbuf[q, at].astype(F32)
+        return cbuf[s, core, at].astype(F32) + sbuf[s, at].astype(F32)
 
     def order(f):
         listed = [(half_ring, f)]
@@ -317,21 +366,34 @@
         copy(ref, ref, sum_send.at[f, j], sum_recv.at[f, j], flows[f]).wait_recv()
         return rbuf[f, j].astype(F32)
 
+    outs = (out_gate, out_up, out_down)
+
+    def own_term(k):
+        if k == 2:
+            value = contract_rows(scaled[:, own_at], acts[...])
+        else:
+            value = contract_rows(
+                tokens_of(list(range(chips)), own_at), grads[:, pl.ds(k * hidden, hidden)]
+            )
+        outs[k][...] = value.astype(BF16)
+
     for j in range(len(order(0))):
         for f in range(2):
             d, h = order(f)[j]
-            value = row_sum(d if f == 0 else -d, h)
+            value = row_sum(slot(1 - f, d), h)
             if (d + 1, h) in order(f):
                 value = value + incoming(f, d, h)
             obuf[f, j] = value.astype(BF16)
             start(obuf.at[f, j], rbuf.at[f, j], sum_send.at[f, j], sum_recv.at[f, j], flows[f])
+        if 1 <= j <= 3:
+            own_term(j - 1)
     for h in range(2):
         value = row_sum(0, h) + incoming(0, 0, h) + incoming(1, 0, h)
         out_tok[pl.ds(h * half, half), :] = value.astype(BF16)
 
-    for k, out in enumerate((out_gate, out_up, out_down)):
+    for k, out in enumerate(outs):
         copy(qbuf.at[k], qbuf.at[k], part_send.at[k], part_recv.at[k], other).wait_recv()
-        out[...] = (term(k, own_rows).astype(F32) + qbuf[k].astype(F32)).astype(BF16)
+        out[...] = (out[...].astype(F32) + qbuf[k].astype(F32)).astype(BF16)
     for op in started:
         op.wait_send()
 
@@ -348,6 +410,8 @@
     numbers = jnp.concatenate([by_expert, total], axis=0).astype(BF16)
 
     messages = chips - 1
+    rows = peers * block
+    early = (chips - 3) * 2 * block
     dma = pltpu.SemaphoreType.DMA
     vmem = pl.BlockSpec(memory_space=pltpu.VMEM)
     outs = pl.pallas_call(
@@ -366,12 +430,15 @@
             pltpu.VMEM((2, messages, block // 2, width), BF16),
             pltpu.VMEM((depth, 2 * hidden), BF16),
             pltpu.VMEM((depth, hidden), BF16),
-            pltpu.VMEM((depth, 2 * hidden), F32),
-            pltpu.VMEM((depth, hidden), F32),
+            pltpu.VMEM((share, 2 * hidden), F32),
+            pltpu.VMEM((share, hidden), F32),
             pltpu.VMEM((3, share, hidden), BF16),
             pltpu.VMEM((3, share, hidden), BF16),
-            pltpu.VMEM((2 * block, width), BF16),
-            pltpu.VMEM((2 * block, 2 * hidden), BF16),
+            pltpu.VMEM((rows, width), BF16),
+            pltpu.VMEM((rows, 2 * hidden), BF16),
+            pltpu.VMEM((rows, hidden), BF16),
+            pltpu.VMEM((early, 2 * hidden), F32),
+            pltpu.VMEM((early, hidden), F32),
             dma((3,)), dma((3,)),
             dma((3, 2, chips // 2)), dma((3, 2, chips // 2)),
             dma((3, chips + 1)), dma((3, chips + 1)),
@@ -380,7 +447,7 @@
             dma((3,)), dma((3,)),
         ],
         compiler_params=pltpu.CompilerParams(
-            collective_id=0, has_side_effects=True, vmem_limit_bytes=56 * 1024 * 1024
+            collective_id=0, has_side_effects=True, vmem_limit_bytes=58 * 1024 * 1024
         ),
         cost_estimate=pl.CostEstimate(
             flops=16 * peers * block * width * hidden, bytes_accessed=8 * block * width, transcendentals=0

time: 92.2 us -> 87.9 us (0.953)
  Pallas kernels: 84.4 us -> 80.1 us
    pallas_call x1, Pallas kernels: 84.4 us -> 80.1 us  [on_device_dense(): pl.pallas_call(functools.partial(layer_kernel, chips), out_shape=(jax.Sha...]
where the time goes in v2:
time: 87.9 us; the launch traced here: 87.6 us
  Pallas kernels  80.1 us (91%)
  local copies, waits for them, and re-layouts  6.09 us (7%)
    pallas_call x1, Pallas kernels, on_device_dense(): pl.pallas_call(functools.partial(layer_kernel, chips), out_shape=(jax.Sha...  80.1 us
    unnamed x14, local copies, waits for them, and re-layouts  6.09 us

profile of v2, /device:TPU:0, one launch (start us, length us, event | category | flops | bytes accessed | tf_op | source)
XLA Modules:
  0.0 87.6 jit_solution(14301017085552760609)
XLA Ops:
  0.6 0.0 copy-start.3
  0.6 0.7 copy-done.3
  1.3 0.0 copy-start.4
  1.4 0.7 copy-done.4
  2.1 0.6 pad_maximum_fusion.num_ref
  2.7 80.1 %shard_map.102 = (bf16[128,1024]{1,0:T(8,128)(2,1)}, bf16[512,384]{1,0:T(8,128)(2,1)}, bf16[512,384]{1,0:T(8,128)(2,1)}, bf16[512,384]{1,0:T(8,128)(2,1)}) custom-call(bf16[128,1024]{1,0:T(8,128)(2,1)} %tok_ref.1, bf16[128,1024]{1,0:T(8,128)(2,1)} %grad_ref.1, bf16[32,128]{1,0:T(8,128)(2,1)} %pad_maximum_fusion.num_ref, bf16[512,384]{1,0:T(8,128)(2,1)} %bitcast.13, ...), custom_call_target="tpu_custom_call" | custom-call | flops 12884901888 | bytes 1048576 | tf_op jit(solution)/shard_map/pallas_call | solution.py:417
  82.8 0.0 copy-start.2
  82.8 1.7 %copy.15 = bf16[128,1024]{1,0:T(8,128)(2,1)} copy(bf16[128,1024]{1,0:T(8,128)(2,1)} %get-tuple-element.16) | data formatting | bytes 524288
  84.5 0.0 copy-done.2
  84.5 0.0 copy-start.1
  84.5 0.7 copy.16
  85.3 0.4 copy-done.1
  85.7 0.0 copy-start
  85.7 0.7 copy.17
  86.4 0.4 copy-done
  86.8 0.7 copy.18
  (5 shorter events, 0.1 us)
Async XLA Ops:
  0.6 0.7 copy-start.3
  1.3 0.7 copy-start.4
  82.8 1.7 %copy-start.2 = (bf16[512,384]{1,0:T(8,128)(2,1)S(1)}, bf16[512,384]{1,0:T(8,128)(2,1)}, u32[]{:S(2)}) copy-start(bf16[512,384]{1,0:T(8,128)(2,1)} %get-tuple-element.9) | copy-start | bytes 1179652
  84.5 1.1 %copy-start.1 = (bf16[512,384]{1,0:T(8,128)(2,1)S(1)}, bf16[512,384]{1,0:T(8,128)(2,1)}, u32[]{:S(2)}) copy-start(bf16[512,384]{1,0:T(8,128)(2,1)} %get-tuple-element.10) | copy-start | bytes 1179652
  85.7 1.1 %copy-start = (bf16[512,384]{1,0:T(8,128)(2,1)S(1)}, bf16[512,384]{1,0:T(8,128)(2,1)}, u32[]{:S(2)}) copy-start(bf16[512,384]{1,0:T(8,128)(2,1)} %get-tuple-element.11) | copy-start | bytes 1179652
